TPU v7x, 128 devices: a whole 4x4x4 slice. The times are simulated.
128 devices in a mesh: gx: 16 (over x, z), gy: 8 (over y, core).
Axes of the slice: x: 4, y: 4, z: 4, core: 2. Of those that a mesh axis runs over, the one named last changes fastest.
Arguments:
- state: float32 [9, 56, 32768], P(None, None, ('gx', 'gy')), may hold values from -6 to 6
- star: float32 [3, 9, 9, 32768], P(None, None, None, ('gx', 'gy')), may hold values from -1.5 to 1.5
- deriv: float32 [3, 56, 56], replicated, may hold values from -0.75 to 0.75
- trace_ops: float32 [4, 56, 21], replicated, may hold values from -0.75 to 0.75
- lift: float32 [4, 21, 56], replicated, may hold values from -1.25 to 1.25
- face_flux: float32 [4, 9, 9, 32768], P(None, None, None, ('gx', 'gy')), may hold values from -0.3 to 0.3
- orient: int32 [4, 32768], P(None, ('gx', 'gy')), may hold values from 0 to 2
- neighbours: int32 [4, 32768], P(None, ('gx', 'gy')), may hold values from 0 to 1536, as said below
- send_faces: int32 [16, 8, 4, 128], P('gx', 'gy'), may hold values from 0 to 1023, as said below
- sea_faces: int32 [16384], P(('gx', 'gy')), may hold values from 0 to 1023
- sea_owner: int32 [16384, 1], P(('gx', 'gy')), may hold values from 0 to 127; in each aligned block of 128 rows (0 to 127, 128 to 255, ...) at most 2 rows name the same one
- sea_blocks: int32 [16384], P(('gx', 'gy')), may hold values from 0 to 255
- sea_weights: float32 [21, 16384, 256], P(None, ('gx', 'gy')), may hold values from -0.6 to 0.6
- depth: float32 [4096, 2048], P('gx', 'gy'), may hold values from 1 to 3
- wet: int32 [4096, 2048], P('gx', 'gy'), may hold values 0 or 1
- sea_state: float32 [3, 4096, 2048], P(None, 'gx', 'gy'), may hold values from -0.6 to 0.6
Outputs:
- elastic: float32 [9, 56, 32768], P(None, None, ('gx', 'gy'))
- ocean: float32 [3, 4096, 2048], P(None, 'gx', 'gy')
Inputs may be any that keep to these rules, and one draw needn't show every extreme that they name: `neighbours`: A code below 1024 names a face of the same device, paired both ways; 1024 + k * 128 + s names the face in slot s of the back-pointing list of the grid neighbour in direction k, which lists this face in its slot s; 1536 marks a face at the edge of the device grid. `send_faces`: local face codes; each face of a device stands in at most one of its lists, once. `sea_faces`: local face codes. `sea_owner`: the flat index of a device, gx index times the gy axis's length plus gy index; among the 128 rows of one device at most 2 name the same owner, and some owner is named 2 times.
All inputs are finite; a program needn't handle non-finite values. No bound on the sum of `wet` on one device may be relied on, other than what follows from the above.
Results may differ from a plain program's by a relative error of at most 0.0001.
Values sent between devices are 32-bit elements; how exact they have to be, the bound alone decides.
A program may use at most 128 MiB of HBM per device.

v0:
```python
import functools
import math

import jax
import jax.numpy as jnp
import numpy as np
from jax import lax
from jax.experimental import pallas as pl
from jax.experimental.pallas import tpu as pltpu
from jax.sharding import PartitionSpec as P

VARS = 9
ORDER = 6
BASIS = 56
NODES = 21
NX, NY = 16, 8
HALF = 32
NPAD = 24
EXT_X, EXT_Y = 264, 384
bf16, f32, i32 = jnp.bfloat16, jnp.float32, jnp.int32
MESH = pl.DeviceIdType.MESH


def turned_nodes():
    upper = ORDER - 1
    nodes = [(i, j) for i in range(upper + 1) for j in range(upper + 1 - i)]
    once = [nodes.index((p[1], upper - p[0] - p[1])) for p in nodes]
    twice = [once[once[n]] for n in range(len(nodes))]
    rest = list(range(NODES, NPAD))
    return np.array(once + rest), np.array(twice + rest)


def filter_matrices():
    k = np.arange(-HALF, HALF + 1)
    raw = 1.0 / np.cosh(math.pi * k / 16.0)
    taps = raw / raw.sum()

    def tap(offset):
        inside = np.abs(offset) <= HALF
        return np.where(inside, taps[np.clip(offset + HALF, 0, 2 * HALF)], 0.0)

    far = 10**6
    cell_x = np.array([r if r < 258 else (r - EXT_X if r >= 262 else far) for r in range(EXT_X)])
    cell_y = np.array([c if c < 258 else (c - EXT_Y if c >= 382 else far) for c in range(EXT_Y)])
    rows_up = np.concatenate([np.arange(0, 32), np.arange(256, 264)])
    rows_down = np.arange(224, 264)
    xs = np.concatenate([cell_x, cell_x[rows_up] + 256, cell_x[rows_down] - 256, np.full(8, far)])
    lane = np.arange(128)
    up = np.where(lane < 64, lane, 256 + lane)
    down = np.where(lane < 64, 256 + lane, 128 + lane)
    ys = np.concatenate([cell_y, cell_y[up] + 256, cell_y[down] - 256])
    column = np.arange(256)
    x_of = (column % 16) * 16 + column // 16
    wx = tap(xs[:, None] - x_of[None, :]).astype(np.float32)
    wy = tap(ys[None, :] - np.arange(256)[:, None]).astype(np.float32)

    def parts(w):
        high = w.astype(jnp.bfloat16)
        low = (w - high.astype(np.float32)).astype(jnp.bfloat16)
        return high, low

    xh, xl = parts(wx)
    yh, yl = parts(wy)
    return np.concatenate([xh, xl], 0), np.concatenate([yh, yl], 1)


def split(x):
    high = x.astype(bf16)
    low = (x - high.astype(f32)).astype(bf16)
    return high, low


def dot(a, b):
    return jnp.dot(a, b, preferred_element_type=f32)


def iota(shape, dim):
    return lax.broadcasted_iota(i32, shape, dim)


def kernel(
    state, star, deriv, trace, lift, flux9, orient, codes, sends, seaf, owner, blocks, weights,
    depth, wet, sea, wx, wy, turns,
    out_el, out_oc,
    star8, flux8, a_op, t_op, l_op, stack, moved, term, integ, base, own, xs, g_out, p_loc, p_arr,
    part, sbuf, arr, xa, fstack, zed, place, disp_t, rows, pay0, pay1, bx0, bx1, my0, my1, by0, by1,
    sel, upl, cont, halo_x, halo_y, halo_c, force, sw, gh_x, gh_y, gh_c, ext,
    orient8, sem_f, sem_x, sem_y, sem_h, sem_g,
):
    gx, gy = lax.axis_index("gx"), lax.axis_index("gy")

    def at(dx, dy):
        return (lax.rem(gx + dx + NX, NX), lax.rem(gy + dy + NY, NY))

    peers = [at(k, 0) for k in range(1, NX)] + [at(0, k) for k in range(1, NY)]
    peers += [at(dx, dy) for dx in (-1, 1) for dy in (-1, 1)]
    barrier = pltpu.get_barrier_semaphore()
    for peer in peers:
        pl.semaphore_signal(barrier, inc=1, device_id=peer, device_id_type=MESH)

    def remote(src, dst, sems, number, peer):
        return pltpu.make_async_remote_copy(
            src_ref=src, dst_ref=dst, send_sem=sems.at[0, number], recv_sem=sems.at[1, number],
            device_id=peer, device_id_type=MESH,
        )

    sw[0:3] = sea[...]
    sw[3] = depth[...]
    sw[4] = wet[...].astype(f32)
    pl.semaphore_wait(barrier, len(peers))
    ghosts = []
    edges_x = {1: pl.ds(248, 8), -1: pl.ds(0, 8)}
    edges_y = {1: pl.ds(128, 128), -1: pl.ds(0, 128)}
    for n, d in enumerate((1, -1)):
        ghosts.append(remote(sw.at[:, edges_x[d], :], gh_x.at[n], sem_g, n, at(d, 0)))
        ghosts.append(remote(sw.at[:, :, edges_y[d]], gh_y.at[n], sem_g, 2 + n, at(0, d)))
        for m, e in enumerate((1, -1)):
            ghosts.append(remote(sw.at[:, edges_x[d], edges_y[e]], gh_c.at[2 * n + m], sem_g, 4 + 2 * n + m, at(d, e)))
    for copy in ghosts:
        copy.start()

    def spread(source, target, sign):
        def body(i, carry):
            block = source[i]
            for v in range(VARS):
                target[i, v] = jnp.broadcast_to(sign * block[v : v + 1, :], (8, 256))
            return carry
        return body

    lax.fori_loop(0, 27, spread(star, star8, -1.0), 0)
    lax.fori_loop(0, 36, spread(flux9, flux8, 1.0), 0)

    for f in range(4):
        orient8[f] = jnp.broadcast_to(orient[f : f + 1, :], (8, 256))

    low_lanes = iota((192, 128), 1) < 64

    def packed(x, mask):
        high, low = split(x)
        high, low = high.astype(f32), low.astype(f32)
        both = jnp.where(mask, high, pltpu.roll(low, 64, 1))
        return jnp.concatenate([both, both], 1).astype(bf16)

    pieces = []
    for d in range(3):
        zed[...] = jnp.zeros((128, 128), f32)
        zed[0:BASIS, 0:BASIS] = deriv[d]
        pieces.append(zed[...].T[0:64])
    a_op[...] = packed(jnp.concatenate(pieces, 0), low_lanes)
    pieces = []
    for f in range(4):
        zed[...] = jnp.zeros((128, 128), f32)
        zed[0:BASIS, 0:NODES] = trace[f]
        pieces.append(zed[...].T[0:NPAD])
    t_op[...] = packed(jnp.concatenate(pieces, 0), low_lanes[0:96])
    zed[...] = jnp.zeros((128, 128), f32)
    for f in range(4):
        zed[32 * f : 32 * f + NODES, 0:BASIS] = lift[f]
    high, low = split(zed[...].T[0:64])
    l_op[0:64] = jnp.concatenate([high, high], 1)
    l_op[64:128] = jnp.concatenate([low, low], 1)

    def hot(target, count, first, lanes, row):
        def body(i, carry):
            here = iota((64, row.shape[1]), 0) + (64 * i + first)
            target[pl.ds(pl.multiple_of(64 * i, 64), 64), lanes] = jnp.where(here == row, 1.0, 0.0).astype(bf16)
            return carry
        lax.fori_loop(0, count // 64, body, 0)

    for k in range(4):
        hot(g_out, 1024, 0, pl.ds(128 * k, 128), sends[k : k + 1, :])
    hot(g_out, 1024, 0, pl.ds(512, 128), seaf[...])
    for f in range(4):
        hot(p_loc, 1024, 0, pl.ds(256 * f, 256), codes[f : f + 1, :])
        hot(p_arr, 512, 1024, pl.ds(256 * f, 256), codes[f : f + 1, :])

    who = owner[...]
    who_t = jnp.broadcast_to(who, (128, 128)).T
    earlier = iota((128, 128), 0) < iota((128, 128), 1)
    rank = jnp.sum(jnp.where((who_t == who) & earlier, 1.0, 0.0), axis=0, keepdims=True).astype(i32)
    spot = (who // 8) * 16 + jnp.where(rank > 0, 8, 0) + lax.rem(who, 8)
    place[...] = jnp.where(iota((256, 128), 0) == spot, 1.0, 0.0).astype(bf16)
    rows[:, 256:384] = jnp.broadcast_to((blocks[...] + 1).astype(f32), (128, 128)).T
    zed[...] = jnp.zeros((128, 128), f32)

    for v in range(VARS):
        term[v, 56:64] = jnp.zeros((8, 256), f32)
        integ[v, 56:64] = jnp.zeros((8, 256), f32)
        base[v, 56:64] = jnp.zeros((8, 256), f32)
    own[216:224] = jnp.zeros((8, 1024), f32)

    def stacked(source):
        def body(v, carry):
            high, low = split(source[v])
            stack[v, 0:64] = high
            stack[v, 64:128] = high
            stack[v, 128:192] = low
            stack[v, 192:256] = low
            return carry
        lax.fori_loop(0, VARS, body, 0)

    def derive(c_integ, c_base, last):
        for v in range(VARS):
            moved[v] = dot(a_op[...], stack[v])

        def body(g, carry):
            at_rows = pl.ds(pl.multiple_of(8 * g, 8), 8)
            for side in range(2):
                lanes = pl.ds(128 * side, 128)
                m = [
                    [moved[v, pl.ds(pl.multiple_of(64 * d + 8 * g, 8), 8), lanes] for d in range(3)]
                    for v in range(VARS)
                ]
                for u in range(VARS):
                    sums = []
                    for d in range(3):
                        acc = m[0][d] * star8[d * 9 + u, 0, :, lanes]
                        for v in range(1, VARS):
                            acc = acc + m[v][d] * star8[d * 9 + u, v, :, lanes]
                        sums.append(acc)
                    acc = sums[0] + sums[1] + sums[2]
                    base[u, at_rows, lanes] = base[u, at_rows, lanes] + c_base * acc
                    if not last:
                        integ[u, at_rows, lanes] = integ[u, at_rows, lanes] + c_integ * acc
                        term[u, at_rows, lanes] = acc
            return carry

        lax.fori_loop(0, 7, body, 0)

    def predict():
        def body(k, carry):
            c_base = jnp.where(k == 1, 1.0, jnp.where(k == 2, 1 / 2, jnp.where(k == 3, 1 / 6, jnp.where(k == 4, 1 / 24, 1 / 120)))).astype(f32)
            c_integ = jnp.where(k == 1, 1 / 2, jnp.where(k == 2, 1 / 6, jnp.where(k == 3, 1 / 24, jnp.where(k == 4, 1 / 120, 1 / 720)))).astype(f32)
            stacked(term)
            derive(c_integ, c_base, False)
            return carry
        lax.fori_loop(1, ORDER, body, 0)
        stacked(integ)
        for v in range(VARS):
            faces = dot(t_op[...], stack[v])
            for f in range(4):
                own[NPAD * v : NPAD * v + NPAD, 256 * f : 256 * f + 256] = faces[NPAD * f : NPAD * f + NPAD]
        high, low = split(own[...])
        xs[0:224] = high
        xs[224:448] = low

    def pick(step):
        got = dot(xs[...], g_out[...])
        got = got[0:224] + got[224:448]
        for k in range(4):
            sbuf[step, k] = got[:, 128 * k : 128 * k + 128]
        zed[0:NPAD] = got[2 * NPAD : 3 * NPAD, 512:640]
        disp_t[...] = zed[...].T

    def project(target):
        def body(i, carry):
            at_rows = pl.ds(pl.multiple_of(32 * i, 32), 32)
            values = disp_t[at_rows]
            acc = values[:, 0:1] * weights[0, at_rows, :]
            for n in range(1, NODES):
                acc = acc + values[:, n : n + 1] * weights[n, at_rows, :]
            rows[at_rows, 0:256] = acc
            return carry
        lax.fori_loop(0, 4, body, 0)
        count = target.shape[0]
        high, low = split(rows[:, 0 : 128 * count])
        placed = dot(place[...], high) + dot(place[...], low)
        for q in range(count):
            target[q] = placed[:, 128 * q : 128 * q + 128]

    directions = ((-1, 0), (1, 0), (0, -1), (0, 1))

    def face_copies(step):
        return [
            remote(sbuf.at[step, k], arr.at[step, k ^ 1], sem_f, 4 * step + k, at(*directions[k]))
            for k in range(4)
        ]

    def x_copies(step, payload, landing):
        slots = pl.ds(pl.multiple_of(16 * gx, 16), 16)
        copies = []
        for k in range(1, NX):
            to = lax.rem(gx + k, NX)
            block = payload.at[:, pl.ds(pl.multiple_of(16 * to, 16), 16), :]
            copies.append(remote(block, landing.at[:, slots, :], sem_x, 15 * step + k - 1, (to, gy)))
        return copies

    def y_copies(step, message, landing):
        copies = []
        for k in range(1, NY):
            to = lax.rem(gy + k, NY)
            copies.append(remote(message.at[to], landing.at[gy], sem_y, 7 * step + k - 1, (gx, to)))
        return copies

    def keep_x(payload, landing):
        slots = pl.ds(pl.multiple_of(16 * gx, 16), 16)
        for q in range(payload.shape[0]):
            landing[q, slots] = payload[q, slots]

    def regroup(landing, message, final):
        for j in range(NY):
            for q in range(landing.shape[0]):
                message[j, q] = landing[q, pl.ds(j, 32, stride=8)]
        final[gy] = message[gy]

    def local_partner():
        got = dot(xs[...], p_loc[...])
        part[...] = got[0:224] + got[224:448]

    def settle(step, target):
        for k in range(4):
            high, low = split(arr[step, k])
            xa[0:224, 128 * k : 128 * k + 128] = high
            xa[224:448, 128 * k : 128 * k + 128] = low
        got = dot(xa[...], p_arr[...])
        part[...] = part[...] + got[0:224] + got[224:448]

        def body(f, carry):
            for side in range(2):
                lanes = pl.ds(128 * side, 128)
                wide = pl.ds(pl.multiple_of(256 * f + 128 * side, 128), 128)
                turn = orient8[f, :, lanes]
                picks = [
                    jnp.where(turn == 0, turns[0, 8 * g : 8 * g + 8], jnp.where(turn == 1, turns[1, 8 * g : 8 * g + 8], turns[2, 8 * g : 8 * g + 8]))
                    for g in range(3)
                ]
                inner = [lax.rem(p, 8) for p in picks]
                jump = []
                for v in range(VARS):
                    source = [part[NPAD * v + 8 * g : NPAD * v + 8 * g + 8, wide] for g in range(3)]
                    jump.append([])
                    for g in range(3):
                        t = [jnp.take_along_axis(s, inner[g], axis=0, mode="promise_in_bounds") for s in source]
                        turned = jnp.where(picks[g] < 8, t[0], jnp.where(picks[g] < 16, t[1], t[2]))
                        jump[v].append(own[NPAD * v + 8 * g : NPAD * v + 8 * g + 8, wide] - turned)
                for u in range(VARS):
                    acc = None
                    for v in range(VARS):
                        w = flux8[f * 9 + u, v, :, lanes]
                        new = [w * jump[v][g] for g in range(3)]
                        acc = new if acc is None else [a + b for a, b in zip(acc, new)]
                    high, low = split(jnp.concatenate(acc + [jnp.zeros((8, 128), f32)], 0))
                    fstack[u, pl.ds(pl.multiple_of(32 * f, 32), 32), lanes] = high
                    fstack[u, pl.ds(pl.multiple_of(128 + 32 * f, 32), 32), lanes] = low
            return carry

        lax.fori_loop(0, 4, body, 0)
        for u in range(VARS):
            s = dot(l_op[...], fstack[u])
            target[u, 0:BASIS] = base[u, 0:BASIS] - (s[0:64] + s[64:128])[0:BASIS]

    def choose(landing):
        labels = landing[:, 2].reshape(256, 128).T[0:1]
        r = iota((256, 256), 0)
        block = lax.rem(r, 16) * 16 + r // 16
        sel[...] = jnp.where(block.astype(f32) + 1.0 == labels, 1.0, 0.0).astype(bf16)

    lane_group = iota((16, 128), 1) // 16

    def contribute(step, landing):
        got = jnp.concatenate([landing[:, q].reshape(256, 128) for q in range(2)], 1)
        high, low = split(got)
        summed = dot(sel[...], high) + dot(sel[...], low)
        for h in range(2):
            half = summed[:, 128 * h : 128 * h + 128]
            turned = [half if s == 0 else pltpu.roll(half, 16 * s, 1) for s in range(8)]
            for j in range(8):
                cx = 8 * h + j
                for hb in range(2):
                    acc = None
                    for b in range(8):
                        block = 8 * hb + b
                        piece = turned[(b - j) % 8][16 * block : 16 * block + 16]
                        acc = piece if acc is None else jnp.where(lane_group == b, piece, acc)
                    upl[16 * cx : 16 * cx + 16, 128 * hb : 128 * hb + 128] = acc
        high, low = split(upl[...])
        first = dot(wx[...], high)
        first = first[0:352] + first[352:704] + dot(wx[0:352], low)
        high, low = split(first)
        cont[step] = dot(high, wy[:, 0:640]) + dot(low, wy[:, 0:640]) + dot(high, wy[:, 640:1280])

    def halo_copies(step):
        copies = []
        x_part = {1: pl.ds(264, 40), -1: pl.ds(304, 40)}
        y_part = {1: pl.ds(384, 128), -1: pl.ds(512, 128)}
        for n, d in enumerate((1, -1)):
            copies.append(remote(cont.at[step, x_part[d], pl.ds(0, 384)], halo_x.at[step, n], sem_h, 8 * step + n, at(d, 0)))
            copies.append(remote(cont.at[step, pl.ds(0, 264), y_part[d]], halo_y.at[step, n], sem_h, 8 * step + 2 + n, at(0, d)))
            for m, e in enumerate((1, -1)):
                copies.append(remote(cont.at[step, x_part[d], y_part[e]], halo_c.at[step, 2 * n + m], sem_h, 8 * step + 4 + 2 * n + m, at(d, e)))
        return copies

    from_x = (gx > 0, gx < NX - 1)
    from_y = (gy > 0, gy < NY - 1)

    def gather_force(step):
        force[...] = cont[step, 0:EXT_X, 0:EXT_Y]

        def add_lanes(row_slice, value, m):
            low = iota(value.shape, 1) < 64
            first, second = jnp.where(low, value, 0.0), jnp.where(low, 0.0, value)
            if m == 0:
                force[row_slice, 0:128] = force[row_slice, 0:128] + first
                force[row_slice, 256:384] = force[row_slice, 256:384] + second
            else:
                force[row_slice, 256:384] = force[row_slice, 256:384] + first
                force[row_slice, 128:256] = force[row_slice, 128:256] + second

        def row_parts(n):
            return ((slice(0, 32), slice(0, 32)), (slice(256, 264), slice(32, 40))) if n == 0 else ((slice(224, 264), slice(0, 40)),)

        for n in range(2):
            value = jnp.where(from_x[n], halo_x[step, n], 0.0)
            for to, of in row_parts(n):
                force[to] = force[to] + value[of]
            add_lanes(slice(0, EXT_X), jnp.where(from_y[n], halo_y[step, n], 0.0), n)
            for m in range(2):
                value = jnp.where(from_x[n] & from_y[m], halo_c[step, 2 * n + m], 0.0)
                for to, of in row_parts(n):
                    add_lanes(to, value[of], m)

    def extend():
        wide = iota((256, 128), 1) < 64
        thin = iota((8, 128), 1) < 64
        upper = iota((8, 256), 0) < 4
        upper_c = iota((8, 128), 0) < 4
        for q in range(5):
            ext[q, 0:256, 0:256] = sw[q]
            minus = jnp.where(from_y[0], gh_y[0, q], 0.0)
            plus = jnp.where(from_y[1], gh_y[1, q], 0.0)
            ext[q, 0:256, 256:384] = jnp.where(wide, plus, minus)
            minus = jnp.where(from_x[0], gh_x[0, q], 0.0)
            plus = jnp.where(from_x[1], gh_x[1, q], 0.0)
            ext[q, 256:264, 0:256] = jnp.where(upper, plus, minus)
            c = [[jnp.where(from_x[n] & from_y[m], gh_c[2 * n + m, q], 0.0) for m in range(2)] for n in range(2)]
            ext[q, 256:264, 256:384] = jnp.where(
                upper_c, jnp.where(thin, c[1][1], c[1][0]), jnp.where(thin, c[0][1], c[0][0])
            )

    def water(eta, us, vs, hold):
        deep, wetf = ext[3], ext[4]
        eta = eta + wetf * force[...]
        column = deep + eta

        def px(a):
            return pltpu.roll(a, EXT_X - 1, 0)

        def mx(a):
            return pltpu.roll(a, 1, 0)

        def py(a):
            return pltpu.roll(a, EXT_Y - 1, 1)

        def my(a):
            return pltpu.roll(a, 1, 1)

        ep, em, en, es = px(eta), mx(eta), py(eta), my(eta)
        up, um, un, us_ = px(us), mx(us), py(us), my(us)
        vp, vm, vn, vs_ = px(vs), mx(vs), py(vs), my(vs)
        qx, qy = column * us, column * vs
        e2 = 0.25 * (ep + em + en + es) - 0.125 * ((px(qx) - mx(qx)) + (py(qy) - my(qy)))
        u2 = 0.25 * (up + um + un + us_) - 0.125 * (us * (up - um) + vs * (un - us_) + (ep - em))
        v2 = 0.25 * (vp + vm + vn + vs_) - 0.125 * (us * (vp - vm) + vs * (vn - vs_) + (en - es))
        hold(0, e2 * wetf)
        hold(1, u2 * wetf)
        hold(2, v2 * wetf)

    def start(copies):
        for copy in copies:
            copy.start()

    def arrive(copies):
        for copy in copies:
            copy.wait()

    def load_field(source):
        for v in range(VARS):
            value = source[v, 0:BASIS]
            term[v, 0:BASIS] = value
            integ[v, 0:BASIS] = value
            base[v, 0:BASIS] = value

    load_field(state)
    predict()
    pick(0)
    faces = face_copies(0)
    start(faces)
    project(pay0)
    xc = x_copies(0, pay0, bx0)
    start(xc)
    keep_x(pay0, bx0)
    stacked(term)
    derive(0.0, 1 / 720, True)
    local_partner()
    arrive(xc)
    regroup(bx0, my0, by0)
    yc0 = y_copies(0, my0, by0)
    start(yc0)
    arrive(faces)
    settle(0, out_el)

    load_field(out_el)
    predict()
    pick(1)
    project(pay1)
    xc = x_copies(1, pay1, bx1)
    start(xc)
    keep_x(pay1, bx1)
    faces = face_copies(1)
    start(faces)
    arrive(yc0)
    choose(by0)
    contribute(0, by0)
    hc0 = halo_copies(0)
    start(hc0)
    arrive(xc)
    regroup(bx1, my1, by1)
    yc1 = y_copies(1, my1, by1)
    start(yc1)
    stacked(term)
    derive(0.0, 1 / 720, True)
    local_partner()
    arrive(ghosts)
    extend()
    arrive(hc0)
    gather_force(0)

    def keep(n, value):
        ext[n] = value

    water(ext[0], ext[1], ext[2], keep)
    arrive(yc1)
    contribute(1, by1)
    hc1 = halo_copies(1)
    start(hc1)
    arrive(faces)
    settle(1, out_el)
    arrive(hc1)
    gather_force(1)

    def emit(n, value):
        out_oc[n] = value[0:256, 0:256]

    water(ext[0], ext[1], ext[2], emit)


def on_device(
    state, star, deriv, trace_ops, lift, face_flux, orient, neighbours, send_faces, sea_faces,
    sea_owner, sea_blocks, sea_weights, depth, wet, sea_state,
):
    wx, wy = filter_matrices()
    once, twice = turned_nodes()
    turns = np.stack([np.arange(NPAD), once, twice]).astype(np.int32)
    turns = np.broadcast_to(turns[:, :, None], (3, NPAD, 128)).copy()
    V = lambda shape, kind=f32: pltpu.VMEM(shape, kind)
    scratch = [
        V((27, 9, 8, 256)), V((36, 9, 8, 256)), V((192, 256), bf16), V((96, 256), bf16), V((128, 256), bf16),
        V((9, 256, 256), bf16), V((9, 192, 256)), V((9, 64, 256)), V((9, 64, 256)), V((9, 64, 256)),
        V((224, 1024)), V((448, 1024), bf16), V((1024, 640), bf16), V((1024, 1024), bf16), V((512, 1024), bf16),
        V((224, 1024)), V((2, 4, 224, 128)), V((2, 4, 224, 128)), V((448, 512), bf16), V((9, 256, 256), bf16),
        V((128, 128)), V((256, 128), bf16), V((128, 128)), V((128, 384)),
        V((3, 256, 128)), V((2, 256, 128)), V((3, 256, 128)), V((2, 256, 128)),
        V((8, 3, 32, 128)), V((8, 2, 32, 128)), V((8, 3, 32, 128)), V((8, 2, 32, 128)),
        V((256, 256), bf16), V((256, 256)), V((2, 352, 640)),
        V((2, 2, 40, 384)), V((2, 2, 264, 128)), V((2, 4, 40, 128)), V((EXT_X, EXT_Y)),
        V((5, 256, 256)), V((2, 5, 8, 256)), V((2, 5, 256, 128)), V((4, 5, 8, 128)), V((5, EXT_X, EXT_Y)),
        V((4, 8, 256), i32),
        pltpu.SemaphoreType.DMA((2, 8)), pltpu.SemaphoreType.DMA((2, 30)), pltpu.SemaphoreType.DMA((2, 14)),
        pltpu.SemaphoreType.DMA((2, 16)), pltpu.SemaphoreType.DMA((2, 8)),
    ]
    ins = [pl.BlockSpec(memory_space=pltpu.VMEM)] * 19
    return pl.pallas_call(
        kernel,
        out_shape=(jax.ShapeDtypeStruct((9, 56, 256), f32), jax.ShapeDtypeStruct((3, 256, 256), f32)),
        in_specs=ins,
        out_specs=(pl.BlockSpec(memory_space=pltpu.VMEM),) * 2,
        scratch_shapes=scratch,
        compiler_params=pltpu.CompilerParams(
            collective_id=0, has_side_effects=True, vmem_limit_bytes=60 * 2**20
        ),
    )(
        state, star.reshape(27, 9, 256), deriv, trace_ops, lift, face_flux.reshape(36, 9, 256), orient,
        neighbours, send_faces.reshape(4, 128), sea_faces.reshape(1, 128), sea_owner.reshape(1, 128),
        sea_blocks.reshape(1, 128), sea_weights, depth, wet, sea_state,
        jnp.asarray(wx), jnp.asarray(wy), jnp.asarray(turns),
    )


def solution(mesh):
    flat = ("gx", "gy")
    placed = (
        P(None, None, flat), P(None, None, None, flat), P(), P(), P(), P(None, None, None, flat), P(None, flat),
        P(None, flat), P("gx", "gy", None, None), P(flat), P(flat, None), P(flat), P(None, flat, None),
        P("gx", "gy"), P("gx", "gy"), P(None, "gx", "gy"),
    )
    return jax.shard_map(
        on_device, mesh=mesh, in_specs=placed,
        out_specs=(P(None, None, flat), P(None, "gx", "gy")), check_vma=False,
    )
```

profile of v0, /device:TPU:1, one launch (start us, length us, event | category | flops | bytes accessed | tf_op | source)
XLA Modules:
  0.0 84.9 jit_solution(4375406309560519085)
XLA Ops:
  0.6 1.4 %copy.24.lift = f32[4,21,56]{2,1,0:T(8,128)} copy(f32[4,21,56]{2,0,1:T(4,128)} %param.23) | data formatting | bytes 37632 | tf_op args[4]
  2.0 1.5 %copy.23.trace = f32[4,56,21]{2,1,0:T(8,128)} copy(f32[4,56,21]{1,0,2:T(4,128)} %param.22) | data formatting | bytes 37632 | tf_op args[3]
  3.6 1.8 %copy.21 = f32[3,9,9,256]{3,2,1,0:T(8,128)} copy(f32[3,9,9,256]{3,0,2,1:T(4,128)} %param.20) | data formatting | bytes 497664 | tf_op args[1]
  5.4 1.9 %copy.22 = f32[4,9,9,256]{3,2,1,0:T(8,128)} copy(f32[4,9,9,256]{3,0,2,1:T(4,128)} %param.24) | data formatting | bytes 663552 | tf_op args[5]
  7.3 73.7 %shard_map.194 = (f32[9,56,256]{2,1,0:T(8,128)}, f32[3,256,256]{2,1,0:T(8,128)}) custom-call(f32[9,56,256]{2,1,0:T(8,128)} %state.1, f32[27,9,256]{2,1,0:T(8,128)} %bitcast.7, f32[3,56,56]{2,1,0:T(8,128)} %deriv.1, f32[4,56,21]{2,1,0:T(8,128)} %copy.23.trace, f32[4,21,56]{2,1,0:T(8,128)} %copy.24.lift, f32[36,9,256]{2,1,0:T(8,128)} %bitcast.6, ...), custom_call_target="tpu_custom_call" | custom-call | tf_op jit(solution)/shard_map/pallas_call | solution.py:572
  81.0 1.9 %copy.27 = f32[9,56,256]{2,1,0:T(8,128)} copy(f32[9,56,256]{2,1,0:T(8,128)} %get-tuple-element.4) | data formatting | bytes 1032192
  82.8 2.1 %copy.28 = f32[3,256,256]{2,1,0:T(8,128)} copy(f32[3,256,256]{2,1,0:T(8,128)} %get-tuple-element.5) | data formatting | bytes 1572864
where the time goes:
time: 86.4 us; the launch traced here: 84.9 us
  Pallas kernels  73.7 us (85%)
  local copies, waits for them, and re-layouts  10.5 us (12%)
    pallas_call x1, Pallas kernels, on_device(): pl.pallas_call(kernel, out_shape=(jax.ShapeDtypeStruct((9, 56, 256), f32)...  73.7 us
    unnamed x6, local copies, waits for them, and re-layouts  10.5 us

commit v1 on v0

--- a/solution.py
+++ b/solution.py
@@ -79,13 +79,15 @@
 
 
 def kernel(
+    state_h, star_h, deriv_h, trace_h, lift_h, flux_h, orient_h, codes_h, sends_h, seaf_h, owner_h, blocks_h, weights_h,
+    depth_h, wet_h, sea_h, wx_h, wy_h, turns_h,
+    out_el, out_oc,
     state, star, deriv, trace, lift, flux9, orient, codes, sends, seaf, owner, blocks, weights,
-    depth, wet, sea, wx, wy, turns,
-    out_el, out_oc,
-    star8, flux8, a_op, t_op, l_op, stack, moved, term, integ, base, own, xs, g_out, p_loc, p_arr,
+    wet, wx, wy, turns, field, water_out, sem_in, sem_out,
+    star8, flux8, a_op, t_op, l_op, stack, istack, moved, integ, base, own, xs, g_out, p_loc, p_arr,
     part, sbuf, arr, xa, fstack, zed, place, disp_t, rows, pay0, pay1, bx0, bx1, my0, my1, by0, by1,
     sel, upl, cont, halo_x, halo_y, halo_c, force, sw, gh_x, gh_y, gh_c, ext,
-    orient8, sem_f, sem_x, sem_y, sem_h, sem_g,
+    orient8, edge_y, sem_f, sem_x, sem_y, sem_h, sem_g,
 ):
     gx, gy = lax.axis_index("gx"), lax.axis_index("gy")
 
@@ -94,6 +96,22 @@
 
     peers = [at(k, 0) for k in range(1, NX)] + [at(0, k) for k in range(1, NY)]
     peers += [at(dx, dy) for dx in (-1, 1) for dy in (-1, 1)]
+    incoming = {}
+    order = (
+        ("star", star_h, star), ("deriv", deriv_h, deriv), ("state", state_h, state), ("trace", trace_h, trace),
+        ("sends", sends_h, sends), ("seaf", seaf_h, seaf), ("owner", owner_h, owner), ("blocks", blocks_h, blocks),
+        ("weights", weights_h, weights), ("codes", codes_h, codes), ("lift", lift_h, lift), ("flux", flux_h, flux9),
+        ("orient", orient_h, orient), ("turns", turns_h, turns), ("sea", sea_h, sw.at[0:3]),
+        ("depth", depth_h, sw.at[3]), ("wet", wet_h, wet), ("wx", wx_h, wx), ("wy", wy_h, wy),
+    )
+    for number, (name, source, target) in enumerate(order):
+        incoming[name] = pltpu.make_async_copy(source, target, sem_in.at[number])
+        incoming[name].start()
+
+    def need(*names):
+        for name in names:
+            incoming[name].wait()
+
     barrier = pltpu.get_barrier_semaphore()
     for peer in peers:
         pl.semaphore_signal(barrier, inc=1, device_id=peer, device_id_type=MESH)
@@ -104,61 +122,47 @@
             device_id=peer, device_id_type=MESH,
         )
 
-    sw[0:3] = sea[...]
-    sw[3] = depth[...]
-    sw[4] = wet[...].astype(f32)
-    pl.semaphore_wait(barrier, len(peers))
-    ghosts = []
-    edges_x = {1: pl.ds(248, 8), -1: pl.ds(0, 8)}
-    edges_y = {1: pl.ds(128, 128), -1: pl.ds(0, 128)}
-    for n, d in enumerate((1, -1)):
-        ghosts.append(remote(sw.at[:, edges_x[d], :], gh_x.at[n], sem_g, n, at(d, 0)))
-        ghosts.append(remote(sw.at[:, :, edges_y[d]], gh_y.at[n], sem_g, 2 + n, at(0, d)))
-        for m, e in enumerate((1, -1)):
-            ghosts.append(remote(sw.at[:, edges_x[d], edges_y[e]], gh_c.at[2 * n + m], sem_g, 4 + 2 * n + m, at(d, e)))
-    for copy in ghosts:
-        copy.start()
-
-    def spread(source, target, sign):
-        def body(i, carry):
-            block = source[i]
+    def spread(source, target, count, sign):
+        def body(u, carry):
+            block = source[u]
             for v in range(VARS):
-                target[i, v] = jnp.broadcast_to(sign * block[v : v + 1, :], (8, 256))
+                for k in range(count):
+                    target[u, v * count + k] = jnp.broadcast_to(sign * block[v, k : k + 1, :], (8, 256))
             return carry
-        return body
-
-    lax.fori_loop(0, 27, spread(star, star8, -1.0), 0)
-    lax.fori_loop(0, 36, spread(flux9, flux8, 1.0), 0)
-
-    for f in range(4):
-        orient8[f] = jnp.broadcast_to(orient[f : f + 1, :], (8, 256))
-
-    low_lanes = iota((192, 128), 1) < 64
-
-    def packed(x, mask):
+        lax.fori_loop(0, VARS, body, 0)
+
+    def packed(x):
         high, low = split(x)
         high, low = high.astype(f32), low.astype(f32)
-        both = jnp.where(mask, high, pltpu.roll(low, 64, 1))
+        both = jnp.where(iota(x.shape, 1) < 64, high, pltpu.roll(low, 64, 1))
         return jnp.concatenate([both, both], 1).astype(bf16)
 
+    need("star", "deriv")
+    spread(star, star8, 3, -1.0)
     pieces = []
+    zed[...] = jnp.zeros((128, 128), f32)
     for d in range(3):
-        zed[...] = jnp.zeros((128, 128), f32)
         zed[0:BASIS, 0:BASIS] = deriv[d]
         pieces.append(zed[...].T[0:64])
-    a_op[...] = packed(jnp.concatenate(pieces, 0), low_lanes)
-    pieces = []
-    for f in range(4):
-        zed[...] = jnp.zeros((128, 128), f32)
-        zed[0:BASIS, 0:NODES] = trace[f]
-        pieces.append(zed[...].T[0:NPAD])
-    t_op[...] = packed(jnp.concatenate(pieces, 0), low_lanes[0:96])
+    a_op[...] = packed(jnp.concatenate(pieces, 0))
+    need("trace")
     zed[...] = jnp.zeros((128, 128), f32)
-    for f in range(4):
-        zed[32 * f : 32 * f + NODES, 0:BASIS] = lift[f]
+    for n in range(NODES):
+        for f in range(4):
+            zed[NPAD * f + n : NPAD * f + n + 1, 0:BASIS] = trace[n, f : f + 1, :]
+    t_op[...] = packed(zed[0:96])
+    need("lift")
+    zed[...] = jnp.zeros((128, 128), f32)
+    for n in range(NODES):
+        for f in range(4):
+            zed[32 * f + n : 32 * f + n + 1, 0:BASIS] = lift[n, f : f + 1, :]
     high, low = split(zed[...].T[0:64])
     l_op[0:64] = jnp.concatenate([high, high], 1)
     l_op[64:128] = jnp.concatenate([low, low], 1)
+    need("flux", "orient", "sends", "seaf", "owner", "blocks", "codes", "turns")
+    spread(flux9, flux8, 4, 1.0)
+    for f in range(4):
+        orient8[f] = jnp.broadcast_to(orient[f : f + 1, :], (8, 256))
 
     def hot(target, count, first, lanes, row):
         def body(i, carry):
@@ -183,61 +187,63 @@
     rows[:, 256:384] = jnp.broadcast_to((blocks[...] + 1).astype(f32), (128, 128)).T
     zed[...] = jnp.zeros((128, 128), f32)
 
-    for v in range(VARS):
-        term[v, 56:64] = jnp.zeros((8, 256), f32)
-        integ[v, 56:64] = jnp.zeros((8, 256), f32)
-        base[v, 56:64] = jnp.zeros((8, 256), f32)
     own[216:224] = jnp.zeros((8, 1024), f32)
 
-    def stacked(source):
+    blank = jnp.zeros((8, 256), f32)
+
+    def load_field(source):
         def body(v, carry):
-            high, low = split(source[v])
-            stack[v, 0:64] = high
-            stack[v, 64:128] = high
-            stack[v, 128:192] = low
-            stack[v, 192:256] = low
+            value = source[v]
+            integ[v] = value
+            base[v] = value
+            hold_split(stack, v, pl.ds(0, 256), jnp.concatenate([value, blank], 0))
             return carry
         lax.fori_loop(0, VARS, body, 0)
+
+    def hold_split(target, v, lanes, value):
+        high, low = split(value)
+        target[v, 0:64, lanes] = high
+        target[v, 64:128, lanes] = high
+        target[v, 128:192, lanes] = low
+        target[v, 192:256, lanes] = low
 
     def derive(c_integ, c_base, last):
         for v in range(VARS):
             moved[v] = dot(a_op[...], stack[v])
 
-        def body(g, carry):
-            at_rows = pl.ds(pl.multiple_of(8 * g, 8), 8)
+        def body(block, carry):
             for side in range(2):
                 lanes = pl.ds(128 * side, 128)
-                m = [
-                    [moved[v, pl.ds(pl.multiple_of(64 * d + 8 * g, 8), 8), lanes] for d in range(3)]
-                    for v in range(VARS)
-                ]
-                for u in range(VARS):
-                    sums = []
+                acc = None
+                for v in range(VARS):
                     for d in range(3):
-                        acc = m[0][d] * star8[d * 9 + u, 0, :, lanes]
-                        for v in range(1, VARS):
-                            acc = acc + m[v][d] * star8[d * 9 + u, v, :, lanes]
-                        sums.append(acc)
-                    acc = sums[0] + sums[1] + sums[2]
-                    base[u, at_rows, lanes] = base[u, at_rows, lanes] + c_base * acc
+                        m = [moved[v, 64 * d + 8 * g : 64 * d + 8 * g + 8, lanes] for g in range(7)]
+                        new = []
+                        for k in range(3):
+                            w = star8[3 * block + k, v * 3 + d, :, lanes]
+                            new += [w * x for x in m]
+                        acc = new if acc is None else [p + q for p, q in zip(acc, new)]
+                for k in range(3):
+                    u = 3 * block + k
+                    value = jnp.concatenate(acc[7 * k : 7 * k + 7], 0)
+                    base[u, :, lanes] = base[u, :, lanes] + c_base * value
                     if not last:
-                        integ[u, at_rows, lanes] = integ[u, at_rows, lanes] + c_integ * acc
-                        term[u, at_rows, lanes] = acc
+                        integ[u, :, lanes] = integ[u, :, lanes] + c_integ * value
+                        hold_split(stack, u, lanes, jnp.concatenate([value, jnp.zeros((8, 128), f32)], 0))
             return carry
 
-        lax.fori_loop(0, 7, body, 0)
+        lax.fori_loop(0, 3, body, 0)
 
     def predict():
         def body(k, carry):
             c_base = jnp.where(k == 1, 1.0, jnp.where(k == 2, 1 / 2, jnp.where(k == 3, 1 / 6, jnp.where(k == 4, 1 / 24, 1 / 120)))).astype(f32)
             c_integ = jnp.where(k == 1, 1 / 2, jnp.where(k == 2, 1 / 6, jnp.where(k == 3, 1 / 24, jnp.where(k == 4, 1 / 120, 1 / 720)))).astype(f32)
-            stacked(term)
             derive(c_integ, c_base, False)
             return carry
         lax.fori_loop(1, ORDER, body, 0)
-        stacked(integ)
         for v in range(VARS):
-            faces = dot(t_op[...], stack[v])
+            hold_split(istack, v, pl.ds(0, 256), jnp.concatenate([integ[v], blank], 0))
+            faces = dot(t_op[...], istack[v])
             for f in range(4):
                 own[NPAD * v : NPAD * v + NPAD, 256 * f : 256 * f + 256] = faces[NPAD * f : NPAD * f + NPAD]
         high, low = split(own[...])
@@ -336,7 +342,7 @@
                 for u in range(VARS):
                     acc = None
                     for v in range(VARS):
-                        w = flux8[f * 9 + u, v, :, lanes]
+                        w = flux8[u, v * 4 + f, :, lanes]
                         new = [w * jump[v][g] for g in range(3)]
                         acc = new if acc is None else [a + b for a, b in zip(acc, new)]
                     high, low = split(jnp.concatenate(acc + [jnp.zeros((8, 128), f32)], 0))
@@ -347,7 +353,7 @@
         lax.fori_loop(0, 4, body, 0)
         for u in range(VARS):
             s = dot(l_op[...], fstack[u])
-            target[u, 0:BASIS] = base[u, 0:BASIS] - (s[0:64] + s[64:128])[0:BASIS]
+            target[u] = base[u] - (s[0:64] + s[64:128])[0:BASIS]
 
     def choose(landing):
         labels = landing[:, 2].reshape(256, 128).T[0:1]
@@ -419,8 +425,24 @@
                 for to, of in row_parts(n):
                     add_lanes(to, value[of], m)
 
+    def ghost_copies():
+        copies = []
+        edges_x = {1: pl.ds(248, 8), -1: pl.ds(0, 8)}
+        edges_y = {1: pl.ds(128, 128), -1: pl.ds(0, 128)}
+        for n, d in enumerate((1, -1)):
+            copies.append(remote(sw.at[:, edges_x[d], :], gh_x.at[n], sem_g, n, at(d, 0)))
+            copies.append(remote(edge_y.at[n], gh_y.at[n], sem_g, 2 + n, at(0, d)))
+            for m, e in enumerate((1, -1)):
+                copies.append(remote(sw.at[:, edges_x[d], edges_y[e]], gh_c.at[2 * n + m], sem_g, 4 + 2 * n + m, at(d, e)))
+        return copies
+
+    def edges():
+        sw[4] = wet[...].astype(f32)
+        for q in range(5):
+            edge_y[0, q] = sw[q, :, 128:256].T[120:128]
+            edge_y[1, q] = sw[q, :, 0:128].T[0:8]
+
     def extend():
-        wide = iota((256, 128), 1) < 64
         thin = iota((8, 128), 1) < 64
         upper = iota((8, 256), 0) < 4
         upper_c = iota((8, 128), 0) < 4
@@ -428,7 +450,8 @@
             ext[q, 0:256, 0:256] = sw[q]
             minus = jnp.where(from_y[0], gh_y[0, q], 0.0)
             plus = jnp.where(from_y[1], gh_y[1, q], 0.0)
-            ext[q, 0:256, 256:384] = jnp.where(wide, plus, minus)
+            middle = jnp.zeros((112, 256), f32)
+            ext[q, 0:256, 256:384] = jnp.concatenate([plus, middle, minus], 0).T
             minus = jnp.where(from_x[0], gh_x[0, q], 0.0)
             plus = jnp.where(from_x[1], gh_x[1, q], 0.0)
             ext[q, 256:264, 0:256] = jnp.where(upper, plus, minus)
@@ -473,33 +496,32 @@
         for copy in copies:
             copy.wait()
 
-    def load_field(source):
-        for v in range(VARS):
-            value = source[v, 0:BASIS]
-            term[v, 0:BASIS] = value
-            integ[v, 0:BASIS] = value
-            base[v, 0:BASIS] = value
-
+    pl.semaphore_wait(barrier, len(peers))
+    need("state")
     load_field(state)
     predict()
     pick(0)
     faces = face_copies(0)
     start(faces)
+    need("weights")
     project(pay0)
     xc = x_copies(0, pay0, bx0)
     start(xc)
     keep_x(pay0, bx0)
-    stacked(term)
     derive(0.0, 1 / 720, True)
     local_partner()
     arrive(xc)
     regroup(bx0, my0, by0)
     yc0 = y_copies(0, my0, by0)
     start(yc0)
+    need("sea", "depth", "wet")
+    edges()
+    ghosts = ghost_copies()
+    start(ghosts)
     arrive(faces)
-    settle(0, out_el)
-
-    load_field(out_el)
+    settle(0, field)
+
+    load_field(field)
     predict()
     pick(1)
     project(pay1)
@@ -508,6 +530,7 @@
     keep_x(pay1, bx1)
     faces = face_copies(1)
     start(faces)
+    need("wx", "wy")
     arrive(yc0)
     choose(by0)
     contribute(0, by0)
@@ -517,7 +540,6 @@
     regroup(bx1, my1, by1)
     yc1 = y_copies(1, my1, by1)
     start(yc1)
-    stacked(term)
     derive(0.0, 1 / 720, True)
     local_partner()
     arrive(ghosts)
@@ -534,14 +556,28 @@
     hc1 = halo_copies(1)
     start(hc1)
     arrive(faces)
-    settle(1, out_el)
+    settle(1, field)
+    elastic_out = pltpu.make_async_copy(field, out_el, sem_out.at[0])
+    elastic_out.start()
     arrive(hc1)
     gather_force(1)
 
     def emit(n, value):
-        out_oc[n] = value[0:256, 0:256]
+        water_out[n] = value[0:256, 0:256]
 
     water(ext[0], ext[1], ext[2], emit)
+    ocean_out = pltpu.make_async_copy(water_out, out_oc, sem_out.at[1])
+    ocean_out.start()
+    elastic_out.wait()
+    ocean_out.wait()
+
+
+def hand_over(a, b, out_a, out_b, sems):
+    copies = [pltpu.make_async_copy(a, out_a, sems.at[0]), pltpu.make_async_copy(b, out_b, sems.at[1])]
+    for copy in copies:
+        copy.start()
+    for copy in copies:
+        copy.wait()
 
 
 def on_device(
@@ -554,8 +590,12 @@
     turns = np.broadcast_to(turns[:, :, None], (3, NPAD, 128)).copy()
     V = lambda shape, kind=f32: pltpu.VMEM(shape, kind)
     scratch = [
-        V((27, 9, 8, 256)), V((36, 9, 8, 256)), V((192, 256), bf16), V((96, 256), bf16), V((128, 256), bf16),
-        V((9, 256, 256), bf16), V((9, 192, 256)), V((9, 64, 256)), V((9, 64, 256)), V((9, 64, 256)),
+        V((9, 56, 256)), V((9, 9, 3, 256)), V((3, 56, 56)), V((21, 4, 56)), V((21, 4, 56)), V((9, 9, 4, 256)),
+        V((4, 256), i32), V((4, 256), i32), V((4, 128), i32), V((1, 128), i32), V((1, 128), i32), V((1, 128), i32),
+        V((21, 128, 256)), V((256, 256), i32), V((704, 256), bf16), V((256, 1280), bf16), V((3, NPAD, 128), i32),
+        V((9, 56, 256)), V((3, 256, 256)), pltpu.SemaphoreType.DMA((19,)), pltpu.SemaphoreType.DMA((2,)),
+        V((9, 27, 8, 256)), V((9, 36, 8, 256)), V((192, 256), bf16), V((96, 256), bf16), V((128, 256), bf16),
+        V((9, 256, 256), bf16), V((9, 256, 256), bf16), V((9, 192, 256)), V((9, 56, 256)), V((9, 56, 256)),
         V((224, 1024)), V((448, 1024), bf16), V((1024, 640), bf16), V((1024, 1024), bf16), V((512, 1024), bf16),
         V((224, 1024)), V((2, 4, 224, 128)), V((2, 4, 224, 128)), V((448, 512), bf16), V((9, 256, 256), bf16),
         V((128, 128)), V((256, 128), bf16), V((128, 128)), V((128, 384)),
@@ -563,27 +603,33 @@
         V((8, 3, 32, 128)), V((8, 2, 32, 128)), V((8, 3, 32, 128)), V((8, 2, 32, 128)),
         V((256, 256), bf16), V((256, 256)), V((2, 352, 640)),
         V((2, 2, 40, 384)), V((2, 2, 264, 128)), V((2, 4, 40, 128)), V((EXT_X, EXT_Y)),
-        V((5, 256, 256)), V((2, 5, 8, 256)), V((2, 5, 256, 128)), V((4, 5, 8, 128)), V((5, EXT_X, EXT_Y)),
-        V((4, 8, 256), i32),
+        V((5, 256, 256)), V((2, 5, 8, 256)), V((2, 5, 8, 256)), V((4, 5, 8, 128)), V((5, EXT_X, EXT_Y)),
+        V((4, 8, 256), i32), V((2, 5, 8, 256)),
         pltpu.SemaphoreType.DMA((2, 8)), pltpu.SemaphoreType.DMA((2, 30)), pltpu.SemaphoreType.DMA((2, 14)),
         pltpu.SemaphoreType.DMA((2, 16)), pltpu.SemaphoreType.DMA((2, 8)),
     ]
-    ins = [pl.BlockSpec(memory_space=pltpu.VMEM)] * 19
-    return pl.pallas_call(
+    place_any = pl.BlockSpec(memory_space=pl.ANY)
+    shapes = (jax.ShapeDtypeStruct((9, 56, 256), f32), jax.ShapeDtypeStruct((3, 256, 256), f32))
+    results = pl.pallas_call(
         kernel,
-        out_shape=(jax.ShapeDtypeStruct((9, 56, 256), f32), jax.ShapeDtypeStruct((3, 256, 256), f32)),
-        in_specs=ins,
-        out_specs=(pl.BlockSpec(memory_space=pltpu.VMEM),) * 2,
+        out_shape=shapes,
+        in_specs=[place_any] * 19,
+        out_specs=(place_any,) * 2,
         scratch_shapes=scratch,
         compiler_params=pltpu.CompilerParams(
             collective_id=0, has_side_effects=True, vmem_limit_bytes=60 * 2**20
         ),
     )(
-        state, star.reshape(27, 9, 256), deriv, trace_ops, lift, face_flux.reshape(36, 9, 256), orient,
+        state, star.transpose(1, 2, 0, 3), deriv, trace_ops.transpose(2, 0, 1), lift.transpose(1, 0, 2),
+        face_flux.transpose(1, 2, 0, 3), orient,
         neighbours, send_faces.reshape(4, 128), sea_faces.reshape(1, 128), sea_owner.reshape(1, 128),
         sea_blocks.reshape(1, 128), sea_weights, depth, wet, sea_state,
         jnp.asarray(wx), jnp.asarray(wy), jnp.asarray(turns),
     )
+    return pl.pallas_call(
+        hand_over, out_shape=shapes, in_specs=[place_any] * 2, out_specs=(place_any,) * 2,
+        scratch_shapes=[pltpu.SemaphoreType.DMA((2,))],
+    )(*results)
 
 
 def solution(mesh):

time: 86.4 us -> 111 us (1.28)
  Pallas kernels: 73.7 us -> 109 us
  local copies, waits for them, and re-layouts: 10.5 us -> 0 us
    pallas_call x1 -> x2, Pallas kernels: 73.7 us -> 109 us  [the longest x1 68.5 us: on_device(): pl.pallas_call(kernel, out_shape=shapes, in_specs=[place_any] * 19, out_s...]
    unnamed x6 -> x0, local copies, waits for them, and re-layouts: 10.5 us -> none
where the time goes in v1:
time: 111 us; the launch traced here: 110 us
  Pallas kernels  109 us (98%)
    pallas_call x1, Pallas kernels, on_device(): pl.pallas_call(kernel, out_shape=shapes, in_specs=[place_any] * 19, out_s...  68.5 us
    pallas_call x1, Pallas kernels, on_device(): pl.pallas_call(hand_over, out_shape=shapes, in_specs=[place_any] * 2, out...  40.6 us

profile of v1, /device:TPU:1, one launch (start us, length us, event | category | flops | bytes accessed | tf_op | source)
XLA Modules:
  0.0 109.9 jit_solution(8176208745496391067)
XLA Ops:
  0.6 68.5 %shard_map.194 = (f32[9,56,256]{2,1,0:T(8,128)}, f32[3,256,256]{2,1,0:T(8,128)}) custom-call(f32[9,56,256]{2,1,0:T(8,128)} %state_h.1, f32[9,9,3,256]{3,2,1,0:T(4,128)} %bitcast.8, f32[3,56,56]{2,1,0:T(8,128)} %deriv_h.1, f32[21,4,56]{2,1,0:T(4,128)} %bitcast.10, f32[21,4,56]{2,1,0:T(4,128)} %bitcast.11, f32[9,9,4,256]{3,2,1,0:T(4,128)} %bitcast.9, ...), custom_call_target="tpu_custom_call" | custom-call | tf_op jit(solution)/shard_map/pallas_call | solution.py:613
  69.1 40.6 %shard_map.195 = (f32[9,56,256]{2,1,0:T(8,128)}, f32[3,256,256]{2,1,0:T(8,128)}) custom-call(f32[9,56,256]{2,1,0:T(8,128)} %get-tuple-element.4.a, f32[3,256,256]{2,1,0:T(8,128)} %get-tuple-element.5.b), custom_call_target="tpu_custom_call" | custom-call | tf_op jit(solution)/shard_map/pallas_call | solution.py:629

commit v2 on v1

--- a/solution.py
+++ b/solution.py
@@ -84,7 +84,7 @@
     out_el, out_oc,
     state, star, deriv, trace, lift, flux9, orient, codes, sends, seaf, owner, blocks, weights,
     wet, wx, wy, turns, field, water_out, sem_in, sem_out,
-    star8, flux8, a_op, t_op, l_op, stack, istack, moved, integ, base, own, xs, g_out, p_loc, p_arr,
+    star8, flux8, a_op, t_op, l_op, stack_a, stack_b, istack, moved_a, moved_b, integ, base, own, xs, g_out, p_loc, p_arr,
     part, sbuf, arr, xa, fstack, zed, place, disp_t, rows, pay0, pay1, bx0, bx1, my0, my1, by0, by1,
     sel, upl, cont, halo_x, halo_y, halo_c, force, sw, gh_x, gh_y, gh_c, ext,
     orient8, edge_y, sem_f, sem_x, sem_y, sem_h, sem_g,
@@ -189,61 +189,71 @@
 
     own[216:224] = jnp.zeros((8, 1024), f32)
 
-    blank = jnp.zeros((8, 256), f32)
+    halves = ((stack_a, moved_a), (stack_b, moved_b))
+    blank = jnp.zeros((8, 128), f32)
+
+    def hold_split(target, lanes, value):
+        high, low = split(jnp.concatenate([value, blank], 0))
+        target[0:64, lanes] = high
+        target[64:128, lanes] = high
+        target[128:192, lanes] = low
+        target[192:256, lanes] = low
 
     def load_field(source):
-        def body(v, carry):
+        for v in range(VARS):
             value = source[v]
             integ[v] = value
             base[v] = value
-            hold_split(stack, v, pl.ds(0, 256), jnp.concatenate([value, blank], 0))
+            for side in range(2):
+                hold_split(halves[side][0], pl.ds(128 * v, 128), value[:, 128 * side : 128 * side + 128])
+        moved_a[...] = dot(a_op[...], stack_a[...])
+
+    def phase(side, c_integ, c_base, last, feed):
+        held, moved = halves[side]
+        other_held, other_moved = halves[1 - side]
+        lanes = pl.ds(128 * side, 128)
+
+        def body(block, carry):
+            if feed:
+                third = pl.ds(pl.multiple_of(384 * block, 128), 384)
+                other_moved[:, third] = dot(a_op[...], other_held[:, third])
+            acc = None
+            for v in range(VARS):
+                for d in range(3):
+                    m = [moved[64 * d + 8 * g : 64 * d + 8 * g + 8, 128 * v : 128 * v + 128] for g in range(7)]
+                    new = []
+                    for k in range(3):
+                        w = star8[3 * block + k, v * 3 + d, :, lanes]
+                        new += [w * x for x in m]
+                    acc = new if acc is None else [p + q for p, q in zip(acc, new)]
+            for k in range(3):
+                u = 3 * block + k
+                value = jnp.concatenate(acc[7 * k : 7 * k + 7], 0)
+                base[u, :, lanes] = base[u, :, lanes] + c_base * value
+                if not last:
+                    integ[u, :, lanes] = integ[u, :, lanes] + c_integ * value
+                    hold_split(held, pl.ds(pl.multiple_of(128 * u, 128), 128), value)
             return carry
-        lax.fori_loop(0, VARS, body, 0)
-
-    def hold_split(target, v, lanes, value):
-        high, low = split(value)
-        target[v, 0:64, lanes] = high
-        target[v, 64:128, lanes] = high
-        target[v, 128:192, lanes] = low
-        target[v, 192:256, lanes] = low
+
+        lax.fori_loop(0, 3, body, 0)
 
     def derive(c_integ, c_base, last):
-        for v in range(VARS):
-            moved[v] = dot(a_op[...], stack[v])
-
-        def body(block, carry):
-            for side in range(2):
-                lanes = pl.ds(128 * side, 128)
-                acc = None
-                for v in range(VARS):
-                    for d in range(3):
-                        m = [moved[v, 64 * d + 8 * g : 64 * d + 8 * g + 8, lanes] for g in range(7)]
-                        new = []
-                        for k in range(3):
-                            w = star8[3 * block + k, v * 3 + d, :, lanes]
-                            new += [w * x for x in m]
-                        acc = new if acc is None else [p + q for p, q in zip(acc, new)]
-                for k in range(3):
-                    u = 3 * block + k
-                    value = jnp.concatenate(acc[7 * k : 7 * k + 7], 0)
-                    base[u, :, lanes] = base[u, :, lanes] + c_base * value
-                    if not last:
-                        integ[u, :, lanes] = integ[u, :, lanes] + c_integ * value
-                        hold_split(stack, u, lanes, jnp.concatenate([value, jnp.zeros((8, 128), f32)], 0))
-            return carry
-
-        lax.fori_loop(0, 3, body, 0)
-
-    def predict():
+        phase(0, c_integ, c_base, last, True)
+        phase(1, c_integ, c_base, last, not last)
+
+    def predict(least, most):
         def body(k, carry):
             c_base = jnp.where(k == 1, 1.0, jnp.where(k == 2, 1 / 2, jnp.where(k == 3, 1 / 6, jnp.where(k == 4, 1 / 24, 1 / 120)))).astype(f32)
             c_integ = jnp.where(k == 1, 1 / 2, jnp.where(k == 2, 1 / 6, jnp.where(k == 3, 1 / 24, jnp.where(k == 4, 1 / 120, 1 / 720)))).astype(f32)
             derive(c_integ, c_base, False)
             return carry
-        lax.fori_loop(1, ORDER, body, 0)
+        lax.fori_loop(least, most, body, 0)
+
+    def traces():
         for v in range(VARS):
-            hold_split(istack, v, pl.ds(0, 256), jnp.concatenate([integ[v], blank], 0))
-            faces = dot(t_op[...], istack[v])
+            for side in range(2):
+                hold_split(istack, pl.ds(256 * v + 128 * side, 128), integ[v, :, 128 * side : 128 * side + 128])
+            faces = dot(t_op[...], istack[:, 256 * v : 256 * v + 256])
             for f in range(4):
                 own[NPAD * v : NPAD * v + NPAD, 256 * f : 256 * f + 256] = faces[NPAD * f : NPAD * f + NPAD]
         high, low = split(own[...])
@@ -499,49 +509,52 @@
     pl.semaphore_wait(barrier, len(peers))
     need("state")
     load_field(state)
-    predict()
+    predict(1, ORDER)
+    traces()
     pick(0)
     faces = face_copies(0)
     start(faces)
+    derive(0.0, 1 / 720, True)
+    local_partner()
     need("weights")
     project(pay0)
+    keep_x(pay0, bx0)
+    arrive(faces)
     xc = x_copies(0, pay0, bx0)
     start(xc)
-    keep_x(pay0, bx0)
-    derive(0.0, 1 / 720, True)
-    local_partner()
+    settle(0, field)
+
+    load_field(field)
+    need("sea", "depth", "wet")
+    edges()
+    ghosts = ghost_copies()
+    start(ghosts)
+    predict(1, 4)
     arrive(xc)
     regroup(bx0, my0, by0)
     yc0 = y_copies(0, my0, by0)
     start(yc0)
-    need("sea", "depth", "wet")
-    edges()
-    ghosts = ghost_copies()
-    start(ghosts)
-    arrive(faces)
-    settle(0, field)
-
-    load_field(field)
-    predict()
+    predict(4, ORDER)
+    traces()
     pick(1)
     project(pay1)
+    arrive(yc0)
     xc = x_copies(1, pay1, bx1)
     start(xc)
     keep_x(pay1, bx1)
-    faces = face_copies(1)
-    start(faces)
     need("wx", "wy")
-    arrive(yc0)
     choose(by0)
     contribute(0, by0)
     hc0 = halo_copies(0)
     start(hc0)
+    derive(0.0, 1 / 720, True)
+    local_partner()
     arrive(xc)
     regroup(bx1, my1, by1)
     yc1 = y_copies(1, my1, by1)
     start(yc1)
-    derive(0.0, 1 / 720, True)
-    local_partner()
+    faces = face_copies(1)
+    start(faces)
     arrive(ghosts)
     extend()
     arrive(hc0)
@@ -572,12 +585,16 @@
     ocean_out.wait()
 
 
-def hand_over(a, b, out_a, out_b, sems):
-    copies = [pltpu.make_async_copy(a, out_a, sems.at[0]), pltpu.make_async_copy(b, out_b, sems.at[1])]
-    for copy in copies:
-        copy.start()
-    for copy in copies:
-        copy.wait()
+def hand_over(a, b, out_a, out_b, hold_a, hold_b, sems):
+    moves = ((a, hold_a), (b, hold_b), (hold_a, out_a), (hold_b, out_b))
+    copies = [pltpu.make_async_copy(source, target, sems.at[n]) for n, (source, target) in enumerate(moves)]
+    copies[0].start()
+    copies[1].start()
+    for n in range(2):
+        copies[n].wait()
+        copies[n + 2].start()
+    copies[2].wait()
+    copies[3].wait()
 
 
 def on_device(
@@ -595,7 +612,7 @@
         V((21, 128, 256)), V((256, 256), i32), V((704, 256), bf16), V((256, 1280), bf16), V((3, NPAD, 128), i32),
         V((9, 56, 256)), V((3, 256, 256)), pltpu.SemaphoreType.DMA((19,)), pltpu.SemaphoreType.DMA((2,)),
         V((9, 27, 8, 256)), V((9, 36, 8, 256)), V((192, 256), bf16), V((96, 256), bf16), V((128, 256), bf16),
-        V((9, 256, 256), bf16), V((9, 256, 256), bf16), V((9, 192, 256)), V((9, 56, 256)), V((9, 56, 256)),
+        V((256, 1152), bf16), V((256, 1152), bf16), V((256, 2304), bf16), V((192, 1152)), V((192, 1152)), V((9, 56, 256)), V((9, 56, 256)),
         V((224, 1024)), V((448, 1024), bf16), V((1024, 640), bf16), V((1024, 1024), bf16), V((512, 1024), bf16),
         V((224, 1024)), V((2, 4, 224, 128)), V((2, 4, 224, 128)), V((448, 512), bf16), V((9, 256, 256), bf16),
         V((128, 128)), V((256, 128), bf16), V((128, 128)), V((128, 384)),
@@ -628,7 +645,7 @@
     )
     return pl.pallas_call(
         hand_over, out_shape=shapes, in_specs=[place_any] * 2, out_specs=(place_any,) * 2,
-        scratch_shapes=[pltpu.SemaphoreType.DMA((2,))],
+        scratch_shapes=[V((9, 56, 256)), V((3, 256, 256)), pltpu.SemaphoreType.DMA((4,))],
     )(*results)
 
 

time: 111 us -> 65.4 us (0.59)
  the two profiles are of different devices: /device:TPU:1 before, /device:TPU:11 now
where the time goes in v2:
time: 65.4 us; the launch traced here: 65.3 us
  Pallas kernels  64.4 us (98%)
  between operations  0.81 us (1%)
    pallas_call x1, Pallas kernels, on_device(): pl.pallas_call(kernel, out_shape=shapes, in_specs=[place_any] * 19, out_s...  62.2 us
    pallas_call x1, Pallas kernels, on_device(): pl.pallas_call(hand_over, out_shape=shapes, in_specs=[place_any] * 2, out...  2.21 us

profile of v2, /device:TPU:11, one launch (start us, length us, event | category | flops | bytes accessed | tf_op | source)
XLA Modules:
  0.0 65.3 jit_solution(12643402111640845543)
XLA Ops:
  0.6 62.2 %shard_map.194 = (f32[9,56,256]{2,1,0:T(8,128)}, f32[3,256,256]{2,1,0:T(8,128)}) custom-call(f32[9,56,256]{2,1,0:T(8,128)} %state_h.1, f32[9,9,3,256]{3,2,1,0:T(4,128)} %bitcast.8, f32[3,56,56]{2,1,0:T(8,128)} %deriv_h.1, f32[21,4,56]{2,1,0:T(4,128)} %bitcast.10, f32[21,4,56]{2,1,0:T(4,128)} %bitcast.11, f32[9,9,4,256]{3,2,1,0:T(4,128)} %bitcast.9, ...), custom_call_target="tpu_custom_call" | custom-call | tf_op jit(solution)/shard_map/pallas_call | solution.py:630
  62.9 2.2 %shard_map.195 = (f32[9,56,256]{2,1,0:T(8,128)}, f32[3,256,256]{2,1,0:T(8,128)}) custom-call(f32[9,56,256]{2,1,0:T(8,128)} %get-tuple-element.4.a, f32[3,256,256]{2,1,0:T(8,128)} %get-tuple-element.5.b), custom_call_target="tpu_custom_call" | custom-call | tf_op jit(solution)/shard_map/pallas_call | solution.py:646

commit v3 on v2

--- a/solution.py
+++ b/solution.py
@@ -85,9 +85,9 @@
     state, star, deriv, trace, lift, flux9, orient, codes, sends, seaf, owner, blocks, weights,
     wet, wx, wy, turns, field, water_out, sem_in, sem_out,
     star8, flux8, a_op, t_op, l_op, stack_a, stack_b, istack, moved_a, moved_b, integ, base, own, xs, g_out, p_loc, p_arr,
-    part, sbuf, arr, xa, fstack, zed, place, disp_t, rows, pay0, pay1, bx0, bx1, my0, my1, by0, by1,
+    part, sbuf, arr, xa, fstack, zed, place, disp_t, rows, pay0, pay1, bx0, bx1, my0, my1, by0, by1, mx0, mx1, fx0, fx1,
     sel, upl, cont, halo_x, halo_y, halo_c, force, sw, gh_x, gh_y, gh_c, ext,
-    orient8, edge_y, sem_f, sem_x, sem_y, sem_h, sem_g,
+    orient8, edge_y, zed_l, sem_f, sem_x, sem_y, sem_h, sem_g,
 ):
     gx, gy = lax.axis_index("gx"), lax.axis_index("gy")
 
@@ -151,19 +151,6 @@
         for f in range(4):
             zed[NPAD * f + n : NPAD * f + n + 1, 0:BASIS] = trace[n, f : f + 1, :]
     t_op[...] = packed(zed[0:96])
-    need("lift")
-    zed[...] = jnp.zeros((128, 128), f32)
-    for n in range(NODES):
-        for f in range(4):
-            zed[32 * f + n : 32 * f + n + 1, 0:BASIS] = lift[n, f : f + 1, :]
-    high, low = split(zed[...].T[0:64])
-    l_op[0:64] = jnp.concatenate([high, high], 1)
-    l_op[64:128] = jnp.concatenate([low, low], 1)
-    need("flux", "orient", "sends", "seaf", "owner", "blocks", "codes", "turns")
-    spread(flux9, flux8, 4, 1.0)
-    for f in range(4):
-        orient8[f] = jnp.broadcast_to(orient[f : f + 1, :], (8, 256))
-
     def hot(target, count, first, lanes, row):
         def body(i, carry):
             here = iota((64, row.shape[1]), 0) + (64 * i + first)
@@ -171,23 +158,39 @@
             return carry
         lax.fori_loop(0, count // 64, body, 0)
 
+    need("sends", "seaf")
     for k in range(4):
         hot(g_out, 1024, 0, pl.ds(128 * k, 128), sends[k : k + 1, :])
     hot(g_out, 1024, 0, pl.ds(512, 128), seaf[...])
-    for f in range(4):
-        hot(p_loc, 1024, 0, pl.ds(256 * f, 256), codes[f : f + 1, :])
-        hot(p_arr, 512, 1024, pl.ds(256 * f, 256), codes[f : f + 1, :])
-
-    who = owner[...]
-    who_t = jnp.broadcast_to(who, (128, 128)).T
-    earlier = iota((128, 128), 0) < iota((128, 128), 1)
-    rank = jnp.sum(jnp.where((who_t == who) & earlier, 1.0, 0.0), axis=0, keepdims=True).astype(i32)
-    spot = (who // 8) * 16 + jnp.where(rank > 0, 8, 0) + lax.rem(who, 8)
-    place[...] = jnp.where(iota((256, 128), 0) == spot, 1.0, 0.0).astype(bf16)
-    rows[:, 256:384] = jnp.broadcast_to((blocks[...] + 1).astype(f32), (128, 128)).T
     zed[...] = jnp.zeros((128, 128), f32)
-
     own[216:224] = jnp.zeros((8, 1024), f32)
+
+    def prepare_surface():
+        need("lift")
+        zed_l[...] = jnp.zeros((128, 128), f32)
+        for n in range(NODES):
+            for f in range(4):
+                zed_l[32 * f + n : 32 * f + n + 1, 0:BASIS] = lift[n, f : f + 1, :]
+        high, low = split(zed_l[...].T[0:64])
+        l_op[0:64] = jnp.concatenate([high, high], 1)
+        l_op[64:128] = jnp.concatenate([low, low], 1)
+        need("flux", "orient", "owner", "blocks", "codes", "turns")
+        spread(flux9, flux8, 4, 1.0)
+        for f in range(4):
+            orient8[f] = jnp.broadcast_to(orient[f : f + 1, :], (8, 256))
+
+        for f in range(4):
+            hot(p_loc, 1024, 0, pl.ds(256 * f, 256), codes[f : f + 1, :])
+            hot(p_arr, 512, 1024, pl.ds(256 * f, 256), codes[f : f + 1, :])
+
+        who = owner[...]
+        who_t = jnp.broadcast_to(who, (128, 128)).T
+        earlier = iota((128, 128), 0) < iota((128, 128), 1)
+        rank = jnp.sum(jnp.where((who_t == who) & earlier, 1.0, 0.0), axis=0, keepdims=True).astype(i32)
+        spot = jnp.where(rank > 0, 128 + lax.rem(who, 8) * 16 + who // 8, who)
+        place[...] = jnp.where(iota((256, 128), 0) == spot, 1.0, 0.0).astype(bf16)
+        rows[:, 256:384] = jnp.broadcast_to((blocks[...] + 1).astype(f32), (128, 128)).T
+
 
     halves = ((stack_a, moved_a), (stack_b, moved_b))
     blank = jnp.zeros((8, 128), f32)
@@ -249,35 +252,41 @@
             return carry
         lax.fori_loop(least, most, body, 0)
 
-    def traces():
-        for v in range(VARS):
+    def traces(variables):
+        for v in variables:
             for side in range(2):
                 hold_split(istack, pl.ds(256 * v + 128 * side, 128), integ[v, :, 128 * side : 128 * side + 128])
             faces = dot(t_op[...], istack[:, 256 * v : 256 * v + 256])
             for f in range(4):
                 own[NPAD * v : NPAD * v + NPAD, 256 * f : 256 * f + 256] = faces[NPAD * f : NPAD * f + NPAD]
+
+    def hold_traces():
         high, low = split(own[...])
         xs[0:224] = high
         xs[224:448] = low
 
+    others = tuple(v for v in range(VARS) if v != 2)
+
     def pick(step):
-        got = dot(xs[...], g_out[...])
+        got = dot(xs[...], g_out[:, 0:512])
         got = got[0:224] + got[224:448]
         for k in range(4):
             sbuf[step, k] = got[:, 128 * k : 128 * k + 128]
-        zed[0:NPAD] = got[2 * NPAD : 3 * NPAD, 512:640]
+
+    def project(target):
+        upward = jnp.concatenate([own[2 * NPAD : 3 * NPAD], jnp.zeros((8, 1024), f32)], 0)
+        high, low = split(upward)
+        got = dot(jnp.concatenate([high, low], 0), g_out[:, 512:640])
+        zed[0:NPAD] = got[0:NPAD] + got[32 : 32 + NPAD]
         disp_t[...] = zed[...].T
 
-    def project(target):
-        def body(i, carry):
-            at_rows = pl.ds(pl.multiple_of(32 * i, 32), 32)
+        for i in range(4):
+            at_rows = pl.ds(32 * i, 32)
             values = disp_t[at_rows]
             acc = values[:, 0:1] * weights[0, at_rows, :]
             for n in range(1, NODES):
                 acc = acc + values[:, n : n + 1] * weights[n, at_rows, :]
             rows[at_rows, 0:256] = acc
-            return carry
-        lax.fori_loop(0, 4, body, 0)
         count = target.shape[0]
         high, low = split(rows[:, 0 : 128 * count])
         placed = dot(place[...], high) + dot(place[...], low)
@@ -292,32 +301,45 @@
             for k in range(4)
         ]
 
-    def x_copies(step, payload, landing):
-        slots = pl.ds(pl.multiple_of(16 * gx, 16), 16)
+    def part_x(k):
+        return pl.ds(pl.multiple_of(8 * k, 8), 8)
+
+    def part_y(k):
+        return pl.ds(pl.multiple_of(128 + 16 * k, 16), 16)
+
+    def first_copies(step, payload, landing):
         copies = []
         for k in range(1, NX):
             to = lax.rem(gx + k, NX)
-            block = payload.at[:, pl.ds(pl.multiple_of(16 * to, 16), 16), :]
-            copies.append(remote(block, landing.at[:, slots, :], sem_x, 15 * step + k - 1, (to, gy)))
-        return copies
-
-    def y_copies(step, message, landing):
-        copies = []
+            copies.append(remote(payload.at[:, part_x(to), :], landing.at[:, part_x(gx), :], sem_x, 30 * step + k - 1, (to, gy)))
         for k in range(1, NY):
             to = lax.rem(gy + k, NY)
-            copies.append(remote(message.at[to], landing.at[gy], sem_y, 7 * step + k - 1, (gx, to)))
+            copies.append(remote(payload.at[:, part_y(to), :], landing.at[:, part_y(gy), :], sem_y, 14 * step + k - 1, (gx, to)))
         return copies
 
-    def keep_x(payload, landing):
-        slots = pl.ds(pl.multiple_of(16 * gx, 16), 16)
+    def second_copies(step, along_y, along_x, final_y, final_x):
+        copies = []
+        for k in range(1, NX):
+            to = lax.rem(gx + k, NX)
+            copies.append(remote(along_x.at[to], final_x.at[gx], sem_x, 30 * step + 15 + k - 1, (to, gy)))
+        for k in range(1, NY):
+            to = lax.rem(gy + k, NY)
+            copies.append(remote(along_y.at[to], final_y.at[gy], sem_y, 14 * step + 7 + k - 1, (gx, to)))
+        return copies
+
+    def keep_own(payload, landing):
         for q in range(payload.shape[0]):
-            landing[q, slots] = payload[q, slots]
-
-    def regroup(landing, message, final):
-        for j in range(NY):
-            for q in range(landing.shape[0]):
-                message[j, q] = landing[q, pl.ds(j, 32, stride=8)]
-        final[gy] = message[gy]
+            landing[q, part_x(gx)] = payload[q, part_x(gx)]
+            landing[q, part_y(gy)] = payload[q, part_y(gy)]
+
+    def regroup(landing, along_y, along_x, final_y, final_x):
+        for q in range(landing.shape[0]):
+            for j in range(NY):
+                along_y[j, q] = landing[q, pl.ds(j, 16, stride=8)]
+            for i in range(NX):
+                along_x[i, q] = landing[q, pl.ds(128 + i, 8, stride=16)]
+        final_y[gy] = along_y[gy]
+        final_x[gx] = along_x[gx]
 
     def local_partner():
         got = dot(xs[...], p_loc[...])
@@ -365,16 +387,19 @@
             s = dot(l_op[...], fstack[u])
             target[u] = base[u] - (s[0:64] + s[64:128])[0:BASIS]
 
-    def choose(landing):
-        labels = landing[:, 2].reshape(256, 128).T[0:1]
+    def landed(final_y, final_x, q):
+        return jnp.concatenate([final_y[:, q].reshape(128, 128), final_x[:, q].reshape(128, 128)], 0)
+
+    def choose(final_y, final_x):
+        labels = landed(final_y, final_x, 2).T[0:1]
         r = iota((256, 256), 0)
         block = lax.rem(r, 16) * 16 + r // 16
         sel[...] = jnp.where(block.astype(f32) + 1.0 == labels, 1.0, 0.0).astype(bf16)
 
     lane_group = iota((16, 128), 1) // 16
 
-    def contribute(step, landing):
-        got = jnp.concatenate([landing[:, q].reshape(256, 128) for q in range(2)], 1)
+    def contribute(step, final_y, final_x):
+        got = jnp.concatenate([landed(final_y, final_x, q) for q in range(2)], 1)
         high, low = split(got)
         summed = dot(sel[...], high) + dot(sel[...], low)
         for h in range(2):
@@ -506,52 +531,56 @@
         for copy in copies:
             copy.wait()
 
-    pl.semaphore_wait(barrier, len(peers))
     need("state")
     load_field(state)
     predict(1, ORDER)
-    traces()
+    traces(range(VARS))
+    hold_traces()
     pick(0)
+    pl.semaphore_wait(barrier, len(peers))
     faces = face_copies(0)
     start(faces)
+    prepare_surface()
     derive(0.0, 1 / 720, True)
     local_partner()
     need("weights")
     project(pay0)
-    keep_x(pay0, bx0)
+    keep_own(pay0, bx0)
+    need("sea", "depth", "wet")
+    edges()
     arrive(faces)
-    xc = x_copies(0, pay0, bx0)
+    xc = first_copies(0, pay0, bx0)
     start(xc)
     settle(0, field)
 
     load_field(field)
-    need("sea", "depth", "wet")
-    edges()
     ghosts = ghost_copies()
     start(ghosts)
     predict(1, 4)
     arrive(xc)
-    regroup(bx0, my0, by0)
-    yc0 = y_copies(0, my0, by0)
+    regroup(bx0, my0, mx0, by0, fx0)
+    yc0 = second_copies(0, my0, mx0, by0, fx0)
     start(yc0)
     predict(4, ORDER)
-    traces()
-    pick(1)
+    traces((2,))
     project(pay1)
     arrive(yc0)
-    xc = x_copies(1, pay1, bx1)
+    xc = first_copies(1, pay1, bx1)
     start(xc)
-    keep_x(pay1, bx1)
+    keep_own(pay1, bx1)
+    traces(others)
+    hold_traces()
+    pick(1)
     need("wx", "wy")
-    choose(by0)
-    contribute(0, by0)
+    choose(by0, fx0)
+    contribute(0, by0, fx0)
     hc0 = halo_copies(0)
     start(hc0)
     derive(0.0, 1 / 720, True)
     local_partner()
     arrive(xc)
-    regroup(bx1, my1, by1)
-    yc1 = y_copies(1, my1, by1)
+    regroup(bx1, my1, mx1, by1, fx1)
+    yc1 = second_copies(1, my1, mx1, by1, fx1)
     start(yc1)
     faces = face_copies(1)
     start(faces)
@@ -565,7 +594,7 @@
 
     water(ext[0], ext[1], ext[2], keep)
     arrive(yc1)
-    contribute(1, by1)
+    contribute(1, by1, fx1)
     hc1 = halo_copies(1)
     start(hc1)
     arrive(faces)
@@ -586,15 +615,20 @@
 
 
 def hand_over(a, b, out_a, out_b, hold_a, hold_b, sems):
-    moves = ((a, hold_a), (b, hold_b), (hold_a, out_a), (hold_b, out_b))
-    copies = [pltpu.make_async_copy(source, target, sems.at[n]) for n, (source, target) in enumerate(moves)]
-    copies[0].start()
-    copies[1].start()
-    for n in range(2):
-        copies[n].wait()
-        copies[n + 2].start()
-    copies[2].wait()
-    copies[3].wait()
+    loads, stores = [], []
+    for source, hold, target, count in ((a, hold_a, out_a, 3), (b, hold_b, out_b, 3)):
+        size = source.shape[0] // count
+        for n in range(count):
+            some, number = pl.ds(size * n, size), len(loads)
+            loads.append(pltpu.make_async_copy(source.at[some], hold.at[some], sems.at[0, number]))
+            stores.append(pltpu.make_async_copy(hold.at[some], target.at[some], sems.at[1, number]))
+    for copy in loads:
+        copy.start()
+    for load, store in zip(loads, stores):
+        load.wait()
+        store.start()
+    for copy in stores:
+        copy.wait()
 
 
 def on_device(
@@ -617,12 +651,13 @@
         V((224, 1024)), V((2, 4, 224, 128)), V((2, 4, 224, 128)), V((448, 512), bf16), V((9, 256, 256), bf16),
         V((128, 128)), V((256, 128), bf16), V((128, 128)), V((128, 384)),
         V((3, 256, 128)), V((2, 256, 128)), V((3, 256, 128)), V((2, 256, 128)),
-        V((8, 3, 32, 128)), V((8, 2, 32, 128)), V((8, 3, 32, 128)), V((8, 2, 32, 128)),
+        V((8, 3, 16, 128)), V((8, 2, 16, 128)), V((8, 3, 16, 128)), V((8, 2, 16, 128)),
+        V((16, 3, 8, 128)), V((16, 2, 8, 128)), V((16, 3, 8, 128)), V((16, 2, 8, 128)),
         V((256, 256), bf16), V((256, 256)), V((2, 352, 640)),
         V((2, 2, 40, 384)), V((2, 2, 264, 128)), V((2, 4, 40, 128)), V((EXT_X, EXT_Y)),
         V((5, 256, 256)), V((2, 5, 8, 256)), V((2, 5, 8, 256)), V((4, 5, 8, 128)), V((5, EXT_X, EXT_Y)),
-        V((4, 8, 256), i32), V((2, 5, 8, 256)),
-        pltpu.SemaphoreType.DMA((2, 8)), pltpu.SemaphoreType.DMA((2, 30)), pltpu.SemaphoreType.DMA((2, 14)),
+        V((4, 8, 256), i32), V((2, 5, 8, 256)), V((128, 128)),
+        pltpu.SemaphoreType.DMA((2, 8)), pltpu.SemaphoreType.DMA((2, 60)), pltpu.SemaphoreType.DMA((2, 28)),
         pltpu.SemaphoreType.DMA((2, 16)), pltpu.SemaphoreType.DMA((2, 8)),
     ]
     place_any = pl.BlockSpec(memory_space=pl.ANY)
@@ -645,7 +680,7 @@
     )
     return pl.pallas_call(
         hand_over, out_shape=shapes, in_specs=[place_any] * 2, out_specs=(place_any,) * 2,
-        scratch_shapes=[V((9, 56, 256)), V((3, 256, 256)), pltpu.SemaphoreType.DMA((4,))],
+        scratch_shapes=[V((9, 56, 256)), V((3, 256, 256)), pltpu.SemaphoreType.DMA((2, 6))],
     )(*results)
 
 

time: 65.4 us -> 61.5 us (0.940)
  the two profiles are of different devices: /device:TPU:11 before, /device:TPU:1 now
where the time goes in v3:
time: 61.5 us; the launch traced here: 61.4 us
  Pallas kernels  60.6 us (99%)
  between operations  0.81 us (1%)
    pallas_call x1, Pallas kernels, on_device(): pl.pallas_call(kernel, out_shape=shapes, in_specs=[place_any] * 19, out_s...  58.4 us
    pallas_call x1, Pallas kernels, on_device(): pl.pallas_call(hand_over, out_shape=shapes, in_specs=[place_any] * 2, out...  2.19 us

profile of v3, /device:TPU:1, one launch (start us, length us, event | category | flops | bytes accessed | tf_op | source)
XLA Modules:
  0.0 61.4 jit_solution(12385480524686168751)
XLA Ops:
  0.6 58.4 %shard_map.194 = (f32[9,56,256]{2,1,0:T(8,128)}, f32[3,256,256]{2,1,0:T(8,128)}) custom-call(f32[9,56,256]{2,1,0:T(8,128)} %state_h.1, f32[9,9,3,256]{3,2,1,0:T(4,128)} %bitcast.8, f32[3,56,56]{2,1,0:T(8,128)} %deriv_h.1, f32[21,4,56]{2,1,0:T(4,128)} %bitcast.10, f32[21,4,56]{2,1,0:T(4,128)} %bitcast.11, f32[9,9,4,256]{3,2,1,0:T(4,128)} %bitcast.9, ...), custom_call_target="tpu_custom_call" | custom-call | tf_op jit(solution)/shard_map/pallas_call | solution.py:665
  59.0 2.2 %shard_map.195 = (f32[9,56,256]{2,1,0:T(8,128)}, f32[3,256,256]{2,1,0:T(8,128)}) custom-call(f32[9,56,256]{2,1,0:T(8,128)} %get-tuple-element.4.a, f32[3,256,256]{2,1,0:T(8,128)} %get-tuple-element.5.b), custom_call_target="tpu_custom_call" | custom-call | tf_op jit(solution)/shard_map/pallas_call | solution.py:681

commit v4 on v3

--- a/solution.py
+++ b/solution.py
@@ -545,26 +545,25 @@
     local_partner()
     need("weights")
     project(pay0)
+    xc = first_copies(0, pay0, bx0)
+    start(xc)
     keep_own(pay0, bx0)
     need("sea", "depth", "wet")
     edges()
     arrive(faces)
-    xc = first_copies(0, pay0, bx0)
-    start(xc)
     settle(0, field)
 
     load_field(field)
     ghosts = ghost_copies()
     start(ghosts)
-    predict(1, 4)
+    predict(1, 3)
     arrive(xc)
     regroup(bx0, my0, mx0, by0, fx0)
     yc0 = second_copies(0, my0, mx0, by0, fx0)
     start(yc0)
-    predict(4, ORDER)
+    predict(3, ORDER)
     traces((2,))
     project(pay1)
-    arrive(yc0)
     xc = first_copies(1, pay1, bx1)
     start(xc)
     keep_own(pay1, bx1)
@@ -572,12 +571,12 @@
     hold_traces()
     pick(1)
     need("wx", "wy")
+    arrive(yc0)
     choose(by0, fx0)
     contribute(0, by0, fx0)
     hc0 = halo_copies(0)
     start(hc0)
     derive(0.0, 1 / 720, True)
-    local_partner()
     arrive(xc)
     regroup(bx1, my1, mx1, by1, fx1)
     yc1 = second_copies(1, my1, mx1, by1, fx1)
@@ -597,6 +596,7 @@
     contribute(1, by1, fx1)
     hc1 = halo_copies(1)
     start(hc1)
+    local_partner()
     arrive(faces)
     settle(1, field)
     elastic_out = pltpu.make_async_copy(field, out_el, sem_out.at[0])

time: 61.5 us -> 60.1 us (0.977)
  Pallas kernels: 60.6 us -> 58.6 us
    pallas_call x1, Pallas kernels: 58.4 us -> 56.4 us  [on_device(): pl.pallas_call(kernel, out_shape=shapes, in_specs=[place_any] * 19, out_s...]
where the time goes in v4:
time: 60.1 us; the launch traced here: 59.4 us
  Pallas kernels  58.6 us (98%)
  between operations  0.81 us (1%)
    pallas_call x1, Pallas kernels, on_device(): pl.pallas_call(kernel, out_shape=shapes, in_specs=[place_any] * 19, out_s...  56.4 us
    pallas_call x1, Pallas kernels, on_device(): pl.pallas_call(hand_over, out_shape=shapes, in_specs=[place_any] * 2, out...  2.19 us

profile of v4, /device:TPU:1, one launch (start us, length us, event | category | flops | bytes accessed | tf_op | source)
XLA Modules:
  0.0 59.4 jit_solution(16795885615818434812)
XLA Ops:
  0.6 56.4 %shard_map.194 = (f32[9,56,256]{2,1,0:T(8,128)}, f32[3,256,256]{2,1,0:T(8,128)}) custom-call(f32[9,56,256]{2,1,0:T(8,128)} %state_h.1, f32[9,9,3,256]{3,2,1,0:T(4,128)} %bitcast.8, f32[3,56,56]{2,1,0:T(8,128)} %deriv_h.1, f32[21,4,56]{2,1,0:T(4,128)} %bitcast.10, f32[21,4,56]{2,1,0:T(4,128)} %bitcast.11, f32[9,9,4,256]{3,2,1,0:T(4,128)} %bitcast.9, ...), custom_call_target="tpu_custom_call" | custom-call | tf_op jit(solution)/shard_map/pallas_call | solution.py:665
  57.1 2.2 %shard_map.195 = (f32[9,56,256]{2,1,0:T(8,128)}, f32[3,256,256]{2,1,0:T(8,128)}) custom-call(f32[9,56,256]{2,1,0:T(8,128)} %get-tuple-element.4.a, f32[3,256,256]{2,1,0:T(8,128)} %get-tuple-element.5.b), custom_call_target="tpu_custom_call" | custom-call | tf_op jit(solution)/shard_map/pallas_call | solution.py:681

commit v5 on v4

--- a/solution.py
+++ b/solution.py
@@ -87,7 +87,7 @@
     star8, flux8, a_op, t_op, l_op, stack_a, stack_b, istack, moved_a, moved_b, integ, base, own, xs, g_out, p_loc, p_arr,
     part, sbuf, arr, xa, fstack, zed, place, disp_t, rows, pay0, pay1, bx0, bx1, my0, my1, by0, by1, mx0, mx1, fx0, fx1,
     sel, upl, cont, halo_x, halo_y, halo_c, force, sw, gh_x, gh_y, gh_c, ext,
-    orient8, edge_y, zed_l, sem_f, sem_x, sem_y, sem_h, sem_g,
+    inner, orient8, edge_y, zed_l, sem_f, sem_x, sem_y, sem_h, sem_g,
 ):
     gx, gy = lax.axis_index("gx"), lax.axis_index("gy")
 
@@ -417,8 +417,20 @@
         high, low = split(upl[...])
         first = dot(wx[...], high)
         first = first[0:352] + first[352:704] + dot(wx[0:352], low)
-        high, low = split(first)
-        cont[step] = dot(high, wy[:, 0:640]) + dot(low, wy[:, 0:640]) + dot(high, wy[:, 640:1280])
+        inner[...] = first[0:272]
+
+        def along_y(value, least, most):
+            high, low = split(value)
+            near = wy[:, least:most]
+            return dot(high, near) + dot(low, near) + dot(high, wy[:, 640 + least : 640 + most])
+
+        cont[step, 0:264, 384:640] = along_y(first[0:272], 384, 640)[0:264]
+        cont[step, 264:352] = along_y(first[256:352], 0, 640)[8:96]
+
+    def contribute_here(step):
+        high, low = split(inner[...])
+        near = wy[:, 0:384]
+        cont[step, 0:264, 0:384] = (dot(high, near) + dot(low, near) + dot(high, wy[:, 640:1024]))[0:264]
 
     def halo_copies(step):
         copies = []
@@ -576,6 +588,7 @@
     contribute(0, by0, fx0)
     hc0 = halo_copies(0)
     start(hc0)
+    contribute_here(0)
     derive(0.0, 1 / 720, True)
     arrive(xc)
     regroup(bx1, my1, mx1, by1, fx1)
@@ -596,6 +609,7 @@
     contribute(1, by1, fx1)
     hc1 = halo_copies(1)
     start(hc1)
+    contribute_here(1)
     local_partner()
     arrive(faces)
     settle(1, field)
@@ -656,7 +670,7 @@
         V((256, 256), bf16), V((256, 256)), V((2, 352, 640)),
         V((2, 2, 40, 384)), V((2, 2, 264, 128)), V((2, 4, 40, 128)), V((EXT_X, EXT_Y)),
         V((5, 256, 256)), V((2, 5, 8, 256)), V((2, 5, 8, 256)), V((4, 5, 8, 128)), V((5, EXT_X, EXT_Y)),
-        V((4, 8, 256), i32), V((2, 5, 8, 256)), V((128, 128)),
+        V((272, 256)), V((4, 8, 256), i32), V((2, 5, 8, 256)), V((128, 128)),
         pltpu.SemaphoreType.DMA((2, 8)), pltpu.SemaphoreType.DMA((2, 60)), pltpu.SemaphoreType.DMA((2, 28)),
         pltpu.SemaphoreType.DMA((2, 16)), pltpu.SemaphoreType.DMA((2, 8)),
     ]

time: 60.1 us -> 59.2 us (0.985)
  no operation moved by 1% of the time
where the time goes in v5:
time: 59.2 us; the launch traced here: 59 us
  Pallas kernels  58.2 us (98%)
  between operations  0.81 us (1%)
    pallas_call x1, Pallas kernels, on_device(): pl.pallas_call(kernel, out_shape=shapes, in_specs=[place_any] * 19, out_s...  56 us
    pallas_call x1, Pallas kernels, on_device(): pl.pallas_call(hand_over, out_shape=shapes, in_specs=[place_any] * 2, out...  2.19 us

profile of v5, /device:TPU:1, one launch (start us, length us, event | category | flops | bytes accessed | tf_op | source)
XLA Modules:
  0.0 59.0 jit_solution(1924029605134088400)
XLA Ops:
  0.6 56.0 %shard_map.194 = (f32[9,56,256]{2,1,0:T(8,128)}, f32[3,256,256]{2,1,0:T(8,128)}) custom-call(f32[9,56,256]{2,1,0:T(8,128)} %state_h.1, f32[9,9,3,256]{3,2,1,0:T(4,128)} %bitcast.8, f32[3,56,56]{2,1,0:T(8,128)} %deriv_h.1, f32[21,4,56]{2,1,0:T(4,128)} %bitcast.10, f32[21,4,56]{2,1,0:T(4,128)} %bitcast.11, f32[9,9,4,256]{3,2,1,0:T(4,128)} %bitcast.9, ...), custom_call_target="tpu_custom_call" | custom-call | tf_op jit(solution)/shard_map/pallas_call | solution.py:679
  56.7 2.2 %shard_map.195 = (f32[9,56,256]{2,1,0:T(8,128)}, f32[3,256,256]{2,1,0:T(8,128)}) custom-call(f32[9,56,256]{2,1,0:T(8,128)} %get-tuple-element.4.a, f32[3,256,256]{2,1,0:T(8,128)} %get-tuple-element.5.b), custom_call_target="tpu_custom_call" | custom-call | tf_op jit(solution)/shard_map/pallas_call | solution.py:695
